TPU v7x, 32 devices: a whole 2x2x4 slice. The times are simulated.
32 devices in a mesh: groups: 2 (over x), ex: 16 (over z, y, core).
Axes of the slice: x: 2, y: 2, z: 4, core: 2. Of those that a mesh axis runs over, the one named last changes fastest.
Arguments:
- acts: bfloat16 [24576, 5120], P(('groups', 'ex')), parts along dimension 0, may hold values from -6 to 6
- grads: bfloat16 [24576, 1024], P(('groups', 'ex')), parts along dimension 0, may hold values from -6 to 6
- domain: int32 [3072], P(('groups', 'ex')), parts along dimension 0, may hold values from 0 to 47
- listed: int32 [32, 2], P(('groups', 'ex')), parts along dimension 0, may hold values 0 or 1
Outputs:
- influence: float32 [3072, 48], P(('groups', 'ex')), parts along dimension 0
There are 2 independent parts, one for each index of `groups`. A program takes and returns all parts, laid end to end along the dimension named above; each array names one. Nothing has to cross between parts.
All inputs are finite; a program needn't handle non-finite values. No bound on the sum of `listed` on one device may be relied on, other than what follows from the above.
Results may differ from a plain program's by a relative error of at most 0.0003.
Values may be sent and summed in bfloat16 or wider, within the bound.
No kernel may reach another device: no remote copies, remote signals or barrier semaphores. Data moves between devices by JAX's collectives and lax.ppermute only.
A program may use at most 192 MiB of HBM per device.

v0:
```python
import functools
import math

import jax
import jax.numpy as jnp
from jax import lax
from jax.experimental import pallas as pl
from jax.experimental.pallas import tpu as pltpu
from jax.sharding import PartitionSpec as P

TOK = 8
TOK_BITS = 3
DOMAINS = 48
LANES = 128
VMEM_BYTES = 63 * 1024 * 1024
LATER_VMEM_BYTES = 44 * 1024 * 1024

INFO = 16

XS, XC, YS, YC, ZS, ZC = range(6)
PAIRS = (
    (YS, XS, 1), (YS, ZS, 1), (YS, XC, 0), (XC, XS, 0),
    (YC, XC, 1), (YC, ZC, 1), (YC, ZS, 0), (YS, ZC, 0), (YC, XS, 0),
)
ONLY = {2: 0, 6: 0, 7: 1, 8: 1}
SLOT = (0, 1, 2, 3, 4, 5, 6, 6, 2)
FIRST = (0, 1, 2, 3)
SMALL = pl.CostEstimate(flops=1, bytes_accessed=1, transcendentals=0)
NT = (((1,), (1,)), ((), ()))
NN = (((1,), (0,)), ((), ()))


def across(chip):
    return chip ^ 1


def along(chip):
    return chip + 2 if chip & 1 else chip - 2


def against(chip):
    return chip - 2 if chip & 1 else chip + 2


def stay(chip):
    return chip


def send(value, move, flip):
    chips = lax.axis_size("ex") // 2
    pairs = [
        (2 * chip + core, 2 * (move(chip) % chips) + (core ^ flip))
        for chip in range(chips)
        for core in range(2)
    ]
    return lax.ppermute(value, "ex", pairs)


def token_major(rows):
    to = lax.broadcasted_iota(jnp.int32, (rows, rows), 0)
    source = lax.broadcasted_iota(jnp.int32, (rows, rows), 1)
    examples = rows // TOK
    place = (source & (TOK - 1)) * examples + lax.shift_right_logical(source, TOK_BITS)
    return (place == to).astype(jnp.bfloat16)


def reorder(order, block):
    return jnp.dot(order, block, preferred_element_type=jnp.float32).astype(jnp.bfloat16)


def put(target, value, info):
    rows = value.shape[0]
    target[:rows, :] = value
    target[rows:, :] = jnp.concatenate([info[...]] * (target.shape[1] // LANES), axis=1)


def chunks(quarter):
    second = quarter // LANES // 2 * LANES
    return quarter - second, second


def cut_kernel(places, info, y_acts, z_acts, y_one, z_one, y_two, z_two, order):
    rows, split = order.shape[0], y_one.shape[1]
    order[...] = token_major(rows)
    put(y_one, reorder(order[...], y_acts[:, :split]), info)
    put(z_one, z_acts[:, :split], info)
    put(y_two, reorder(order[...], y_acts[:, split:]), info)
    put(z_two, z_acts[:, split:], info)


def cut(acts, info, places):
    rows, width = acts.shape
    quarter = width // 4
    one, two = chunks(quarter)
    shapes = [(rows + INFO, one)] * 2 + [(rows + INFO, two)] * 2
    return pl.pallas_call(
        cut_kernel,
        grid_spec=pltpu.PrefetchScalarGridSpec(
            num_scalar_prefetch=1,
            grid=(1,),
            in_specs=[
                pl.BlockSpec((INFO, LANES), lambda i, p: (0, 0)),
                pl.BlockSpec((rows, quarter), lambda i, p: (0, p[0])),
                pl.BlockSpec((rows, quarter), lambda i, p: (0, p[1])),
            ],
            out_specs=[pl.BlockSpec(shape, lambda i, p: (0, 0)) for shape in shapes],
            scratch_shapes=[pltpu.VMEM((rows, rows), jnp.bfloat16)],
        ),
        out_shape=[jax.ShapeDtypeStruct(shape, acts.dtype) for shape in shapes],
        compiler_params=pltpu.CompilerParams(vmem_limit_bytes=VMEM_BYTES),
        cost_estimate=SMALL,
        name="cut",
    )(places, info, acts, acts)


def half_kernel(steps, place, info, acts, grads, out):
    @pl.when(pl.program_id(0) < steps)
    def _():
        put(out, acts[...], info)

    @pl.when(pl.program_id(0) >= steps)
    def _():
        put(out, grads[...], info)


def cut_half(acts, grads, info, place):
    rows, width = acts.shape
    half, depth = width // 2, grads.shape[1]
    step = math.gcd(math.gcd(half, depth), 512)
    steps = half // step
    return pl.pallas_call(
        functools.partial(half_kernel, steps),
        grid_spec=pltpu.PrefetchScalarGridSpec(
            num_scalar_prefetch=1,
            grid=(steps + depth // step,),
            in_specs=[
                pl.BlockSpec((INFO, LANES), lambda i, p: (0, 0)),
                pl.BlockSpec((rows, step), lambda i, p: (0, p[0] * steps + jnp.minimum(i, steps - 1))),
                pl.BlockSpec((rows, step), lambda i, p: (0, jnp.maximum(i - steps, 0))),
            ],
            out_specs=pl.BlockSpec((rows + INFO, step), lambda i, p: (0, i)),
        ),
        out_shape=jax.ShapeDtypeStruct((rows + INFO, half + depth), acts.dtype),
        compiler_params=pltpu.CompilerParams(vmem_limit_bytes=VMEM_BYTES),
        cost_estimate=SMALL,
        name="half",
    )(place, info, acts, grads)


def guarded(pair, mirrored, work):
    if pair in ONLY:
        pl.when(mirrored == ONLY[pair])(work)
    else:
        work()


def grams_kernel(flags, xs, xc, ys, yc, zs, zc, out, held, result, in_sems, out_sems):
    mirrored = flags[0]
    rows, depth = xs.shape
    order = token_major(rows)
    sources = (xs, xc.at[:rows, xc.shape[1] - depth:], ys, yc, zs, zc)
    loads = [
        pltpu.make_async_copy(source, held.at[at], in_sems.at[at])
        for at, source in enumerate(sources)
    ]
    for block in (YS, XS, ZS, XC, YC, ZC):
        loads[block].start()
    here = set()

    def ready(*blocks):
        for block in blocks:
            if block not in here:
                here.add(block)
                loads[block].wait()
                if block in (YS, YC):
                    held[block] = reorder(order, held[block])

    for pair, (one, two, _) in enumerate(PAIRS):
        ready(one, two)
        slot = SLOT[pair]

        def work(one=one, two=two, slot=slot):
            result[slot] = lax.dot_general(
                held[one], held[two], NT, preferred_element_type=jnp.float32
            )
            pltpu.make_async_copy(result.at[slot], out.at[slot], out_sems.at[slot]).start()

        guarded(pair, mirrored, work)
    for slot in range(7):
        pltpu.make_async_copy(result.at[slot], out.at[slot], out_sems.at[slot]).wait()


def grams(flags, grads, *messages):
    rows, width = grads.shape
    return pl.pallas_call(
        grams_kernel,
        in_specs=[pl.BlockSpec(memory_space=pltpu.SMEM)] + [pl.BlockSpec(memory_space=pl.ANY)] * 6,
        out_specs=pl.BlockSpec(memory_space=pl.ANY),
        out_shape=jax.ShapeDtypeStruct((7, rows, rows), jnp.float32),
        scratch_shapes=[
            pltpu.VMEM((6, rows, width), grads.dtype),
            pltpu.VMEM((7, rows, rows), jnp.float32),
            pltpu.SemaphoreType.DMA((6,)),
            pltpu.SemaphoreType.DMA((7,)),
        ],
        compiler_params=pltpu.CompilerParams(vmem_limit_bytes=VMEM_BYTES),
        cost_estimate=SMALL,
        name="grams",
    )(flags, grads, *messages)


def product(one, two, inner):
    rows = inner.shape[0]
    inner[...] = lax.dot_general(
        one[:rows, :], two[:rows, :], NT, preferred_element_type=jnp.float32
    )


def token_sums(inner, gram, sums, ordered=True):
    examples, rows = sums.shape
    if ordered:
        sums[...] = sum(
            inner[at:at + examples, :] * gram[at:at + examples, :]
            for at in range(0, rows, examples)
        )
    else:
        weighted = inner[...] * gram[...]
        sums[...] = weighted.reshape(examples, TOK, rows).sum(axis=1)


def two_parts(value):
    high = value.astype(jnp.bfloat16)
    return high, (value - high.astype(jnp.float32)).astype(jnp.bfloat16)


def dot_parts(value, table):
    high, low = two_parts(value)
    return lax.dot_general(low, table, NT, preferred_element_type=jnp.float32) + lax.dot_general(
        high, table, NT, preferred_element_type=jnp.float32
    )


def side_by_side(values):
    return jnp.concatenate(values, axis=1)


def domain_sums(pairs, factor, place, info, sums):
    count, examples, rows = sums.shape
    example = lax.broadcasted_iota(jnp.int32, (LANES, rows), 0)
    column = lax.broadcasted_iota(jnp.int32, (LANES, rows), 1)
    gather = (lax.shift_right_logical(column, TOK_BITS) == example).astype(jnp.bfloat16)
    tiles = dot_parts(sums[...].reshape(count * examples, rows), gather)
    tiles = tiles.reshape(count, examples, LANES)
    mirrored, core, side = place
    lane = lax.broadcasted_iota(jnp.int32, (1, LANES), 1)
    row = lax.broadcasted_iota(jnp.int32, (DOMAINS, LANES), 0)
    hot = {
        block: ((value.astype(jnp.int32) == row) & (lane < examples)).astype(jnp.bfloat16)
        for block, value in info.items()
    }

    def listed_flag(block, apart):
        return jnp.sum(jnp.where(lane == examples + apart, info[block], 0.0), axis=1, keepdims=True)

    pad = jnp.zeros((LANES - examples, LANES), jnp.float32)
    groups = {}
    for at, pair in pairs:
        one, two, apart = PAIRS[pair]
        if one == XC:
            two_leads = core == 0
        elif two in (XS, XC):
            two_leads = side == 0
        else:
            two_leads = side == 1
        flag = jnp.where(two_leads, listed_flag(two, apart), listed_flag(one, apart))
        if pair in ONLY:
            flag = jnp.where(mirrored == ONLY[pair], flag, 0.0)
        tile = jnp.concatenate([tiles[at], pad], axis=0) * (flag * factor)
        groups.setdefault(one, []).append((two, *two_parts(tile)))
    total = {}

    def add(block, term):
        total[block] = total[block] + term if block in total else term

    for one, group in groups.items():
        others = side_by_side([hot[two] for two, _, _ in group])
        highs = side_by_side([high for _, high, _ in group])
        lows = side_by_side([low for _, _, low in group])
        add(one, lax.dot_general(
            side_by_side([others, others]), side_by_side([highs, lows]), NT,
            preferred_element_type=jnp.float32,
        ))
        columns_of = lax.dot_general(
            side_by_side([hot[one], hot[one]]), jnp.concatenate([highs, lows], axis=0), NN,
            preferred_element_type=jnp.float32,
        )
        for at, (two, _, _) in enumerate(group):
            add(two, columns_of[:, at * LANES:(at + 1) * LANES])
    return total


def copies_of(loads, sems):
    return {
        key: pltpu.make_async_copy(source, target, sems.at[at])
        for at, (key, (source, target)) in enumerate(loads.items())
    }


def start(copies, *keys):
    for key in keys:
        copies[key].start()


def wait(copies, *keys):
    for key in keys:
        copies[key].wait()


def info_row(notes, block):
    return notes[block].astype(jnp.float32)[:1]


def columns(ref, at, width):
    return ref.at[:, pl.ds(pl.multiple_of(at, LANES), width)]


def first_kernel(factor, flags, own_info, acts, x_half, ys_one, zs_one, ys_two, zs_two, gram, out, notes,
                 xs_v, xc_v, ys_v, zs_v, own_v, half_v, gram_v, inner, sums, sems):
    half_at, in_half, work_at = flags[1], flags[2], flags[5]
    quarter = xs_v.shape[1]
    split = ys_one.shape[1]
    rows = inner.shape[1]
    copies = copies_of({
        "xs": (columns(acts, work_at, quarter), xs_v),
        "ys": (ys_one, ys_v.at[:, :split]),
        "ys2": (ys_two, ys_v.at[:, split:]),
        "g0": (gram.at[0], gram_v.at[0]),
        "zs": (zs_one, zs_v.at[:, :split]),
        "zs2": (zs_two, zs_v.at[:, split:]),
        "g1": (gram.at[1], gram_v.at[1]),
        "xc": (columns(x_half, in_half, quarter), xc_v),
        "g2": (gram.at[2], gram_v.at[2]),
        "own": (columns(acts, half_at, 2 * quarter), own_v),
        "half": (x_half.at[:, :2 * quarter], half_v),
        "g3": (gram.at[3], gram_v.at[3]),
    }, sems)
    start(copies, "xs", "ys", "ys2", "g0")
    wait(copies, "xs", "ys", "ys2")
    start(copies, "zs", "zs2", "g1", "xc", "g2")
    product(ys_v, xs_v, inner.at[0])
    wait(copies, "g0", "zs", "zs2", "xc")
    product(ys_v, zs_v, inner.at[1])
    token_sums(inner.at[0], gram_v.at[0], sums.at[0])
    start(copies, "own", "half", "g3")
    wait(copies, "g1", "g2")
    product(ys_v, xc_v, inner.at[0])
    token_sums(inner.at[1], gram_v.at[1], sums.at[1])
    wait(copies, "own", "half")
    product(half_v, own_v, inner.at[1])
    token_sums(inner.at[0], gram_v.at[2], sums.at[2])
    wait(copies, "g3")
    token_sums(inner.at[1], gram_v.at[3], sums.at[3], ordered=False)
    notes[...] = jnp.zeros_like(notes)
    notes[XS] = own_info[...]
    notes[XC] = xc_v[rows:, :LANES]
    notes[YS] = ys_v[rows:, split:split + LANES]
    notes[ZS] = zs_v[rows:, split:split + LANES]
    info = {block: info_row(notes, block) for block in (XS, XC, YS, ZS)}
    place = flags[0], flags[3], flags[4]
    total = domain_sums(tuple(enumerate(FIRST)), factor, place, info, sums)
    out[...] = jnp.zeros_like(out)
    for block, value in total.items():
        out[block] = value


def position():
    me = lax.axis_index("ex")
    return me & 1, lax.shift_right_logical(me, 1) & 1


def later_kernel(factor, at, notes, earlier, *refs):
    (acts, x_half, ys, yc, zs, zc, gram), refs = refs[:7], refs[7:]
    outs, (held, notes_v, earlier_v, gram_v, inner, sums, sems) = refs[:-7], refs[-7:]
    rows, width = inner.shape[1], held.shape[2]
    quarter = acts.shape[1] // 4
    core, side = position()
    mirrored = core ^ side
    in_half = (1 - side) * quarter
    work_at = core * 2 * quarter + in_half
    copies = copies_of({
        XS: (columns(acts, work_at + at, width), held.at[XS, :rows, :]),
        XC: (columns(x_half, in_half + at, width), held.at[XC]),
        YS: (ys, held.at[YS, :ys.shape[0], :]),
        YC: (yc, held.at[YC, :yc.shape[0], :]),
        ZS: (zs, held.at[ZS, :zs.shape[0], :]),
        ZC: (zc, held.at[ZC, :zc.shape[0], :]),
        "g4": (gram.at[4], gram_v.at[0]),
        "g5": (gram.at[5], gram_v.at[1]),
        "g6": (gram.at[6], gram_v.at[2]),
        "g2": (gram.at[2], gram_v.at[3]),
        "notes": (notes, notes_v),
        "earlier": (earlier, earlier_v),
    }, sems)
    start(copies, YC, XC, ZC)
    wait(copies, YC, XC)
    start(copies, "g4", YS, ZS)
    product(held.at[YC], held.at[XC], inner.at[0])
    wait(copies, ZC)
    start(copies, "g5", XS)
    product(held.at[YC], held.at[ZC], inner.at[1])
    wait(copies, "g4", YS, ZS)
    start(copies, "g6", "g2", "notes", "earlier")
    token_sums(inner.at[0], gram_v.at[0], sums.at[0])
    product(held.at[jnp.where(mirrored == 0, YC, YS)], held.at[jnp.where(mirrored == 0, ZS, ZC)], inner.at[0])
    wait(copies, "g5", XS)
    token_sums(inner.at[1], gram_v.at[1], sums.at[1])
    wait(copies, "g6", "g2", "notes", "earlier")

    @pl.when(mirrored == 1)
    def _():
        product(held.at[YC], held.at[XS], inner.at[1])
        token_sums(inner.at[0], gram_v.at[2], sums.at[2])
        token_sums(inner.at[1], gram_v.at[3], sums.at[3])

    @pl.when(mirrored == 0)
    def _():
        token_sums(inner.at[0], gram_v.at[2], sums.at[2])
        sums[3] = jnp.zeros(sums.shape[1:], jnp.float32)

    if at == 0:
        total_out, notes_out = outs
        for block in (YC, ZC):
            notes_v[block] = held[block, rows:, :LANES]
        notes_out[...] = notes_v[...]
    info = {block: info_row(notes_v, block) for block in range(6)}
    pairs = ((0, 4), (1, 5), (2, 6), (2, 7), (3, 8))
    total = domain_sums(pairs, factor, (mirrored, core, side), info, sums)
    examples = sums.shape[1]
    for block, value in total.items():
        value = value + earlier_v[block]
        if at == 0:
            total_out[block] = value
        else:
            outs[block][...] = value[:, :examples]


def per_device(acts, grads, domain, listed):
    rows, width = acts.shape
    examples = rows // TOK
    quarter = width // 4
    me = lax.axis_index("ex")
    core = me % 2
    side = (me // 2) % 2
    mirrored = core ^ side

    flags = jnp.stack([
        mirrored, core * 2 * quarter, (1 - side) * quarter, core, side,
        core * 2 * quarter + (1 - side) * quarter,
    ]).astype(jnp.int32)
    places = jnp.stack([core * 2 + side, core * 2 + (1 - side)]).astype(jnp.int32)
    cross_places = jnp.stack([(1 - core) * 2 + side, (1 - core) * 2 + (1 - side)]).astype(jnp.int32)
    half_place = jnp.stack([1 - core]).astype(jnp.int32)

    own_info = jnp.concatenate(
        [domain, listed[0], jnp.zeros((LANES - examples - 2,), jnp.int32)]
    )
    own_info = jnp.broadcast_to(own_info.astype(acts.dtype)[None, :], (INFO, LANES))

    grads_ys = send(grads, across, 0)
    grads_zs = send(grads, along, 0)
    cut_ys, cut_zs, cut_ys_two, cut_zs_two = cut(acts, own_info, places)
    own_info, _ = lax.optimization_barrier((own_info, cut_ys))
    cut_yc, cut_zc, cut_yc_two, cut_zc_two = cut(acts, own_info, cross_places)
    own_info, _ = lax.optimization_barrier((own_info, cut_yc))
    ys_one = send(cut_ys, across, 0)
    zs_one = send(cut_zs, along, 0)
    ys_two = send(cut_ys_two, across, 0)
    zs_two = send(cut_zs_two, along, 0)
    yc_one = send(cut_yc, across, 1)
    zc_one = send(cut_zc, along, 1)
    yc_two = send(cut_yc_two, across, 1)

    def exchange(*values):
        return lax.cond(
            listed[0, 0] < 2,
            lambda *sent: tuple(send(value, stay, 1) for value in sent),
            lambda *sent: tuple(jnp.zeros_like(value) for value in sent),
            *values,
        )

    x_half, = exchange(cut_half(acts, grads, own_info, half_place))
    grads_ys, grads_zs, x_half = lax.optimization_barrier((grads_ys, grads_zs, x_half))
    grads_yc, grads_zc = exchange(grads_ys, grads_zs)
    factor = 1.0 / (TOK * math.sqrt(width * grads.shape[1]))

    grads_yc, ys_one, zs_one = lax.optimization_barrier((grads_yc, ys_one, zs_one))
    gram = grams(flags, grads, x_half, grads_ys, grads_yc, grads_zs, grads_zc)
    cut_zc_two, gram = lax.optimization_barrier((cut_zc_two, gram))
    zc_two = send(cut_zc_two, along, 1)

    smem = pl.BlockSpec(memory_space=pltpu.SMEM)
    vmem = pl.BlockSpec(memory_space=pltpu.VMEM)
    hbm = pl.BlockSpec(memory_space=pl.ANY)
    params = pltpu.CompilerParams(vmem_limit_bytes=VMEM_BYTES)
    own_v = pltpu.VMEM((rows, quarter), acts.dtype)
    slice_v = pltpu.VMEM((rows + INFO, quarter), acts.dtype)
    shared = [
        pltpu.VMEM((4, rows, rows), jnp.float32),
        pltpu.VMEM((2, rows, rows), jnp.float32),
        pltpu.VMEM((4, examples, rows), jnp.float32),
    ]
    partial_sums = jax.ShapeDtypeStruct((6, DOMAINS, LANES), jnp.float32)
    all_notes = jax.ShapeDtypeStruct((6, INFO, LANES), acts.dtype)
    first, notes = pl.pallas_call(
        functools.partial(first_kernel, factor),
        in_specs=[smem, vmem] + [hbm] * 7,
        out_specs=[vmem, vmem],
        out_shape=[partial_sums, all_notes],
        scratch_shapes=[own_v] + [slice_v] * 3 + [
            pltpu.VMEM((rows, 2 * quarter), acts.dtype),
            pltpu.VMEM((rows + INFO, 2 * quarter), acts.dtype),
        ] + shared + [pltpu.SemaphoreType.DMA((12,))],
        compiler_params=params,
        cost_estimate=SMALL,
        name="first",
    )(flags, own_info, acts, x_half, ys_one, zs_one, ys_two, zs_two, gram)

    def later(at, notes, earlier, messages, out_shape):
        return pl.pallas_call(
            functools.partial(later_kernel, factor, at),
            in_specs=[hbm] * 9,
            out_specs=[vmem] * len(out_shape),
            out_shape=out_shape,
            scratch_shapes=[
                pltpu.VMEM((6, rows + INFO, messages[0].shape[1]), acts.dtype),
                pltpu.VMEM(all_notes.shape, acts.dtype),
                pltpu.VMEM(partial_sums.shape, jnp.float32),
            ] + shared + [pltpu.SemaphoreType.DMA((12,))],
            compiler_params=pltpu.CompilerParams(vmem_limit_bytes=LATER_VMEM_BYTES),
            cost_estimate=SMALL,
            name="later",
        )(notes, earlier, acts, x_half, *messages, gram)

    second, notes = later(
        0, notes, first, (ys_one, yc_one, zs_one, zc_one),
        [partial_sums, all_notes],
    )
    sums = later(
        ys_one.shape[1], notes, second, (ys_two, yc_two, zs_two, zc_two),
        [jax.ShapeDtypeStruct((DOMAINS, examples), jnp.float32)] * 6,
    )

    total = sums[XS]
    total = total + send(sums[XC], stay, 1)
    total = total + send(sums[YS], across, 0)
    total = total + send(sums[YC], across, 1)
    total = total + send(sums[ZS], against, 0)
    total = total + send(sums[ZC], against, 1)
    return total.T


def solution(mesh):
    in_specs = (
        P(("groups", "ex"), None),
        P(("groups", "ex"), None),
        P(("groups", "ex")),
        P(("groups", "ex"), None),
    )
    out_specs = P(("groups", "ex"), None)
    return jax.shard_map(
        per_device, mesh=mesh, in_specs=in_specs, out_specs=out_specs, check_vma=False
    )
```

profile of v0, /device:TPU:0, one launch (start us, length us, event | category | flops | bytes accessed | tf_op | source)
XLA Modules:
  0.0 144.2 jit_solution(7395974374450531953)
XLA Ops:
  0.0 5.0 %collective-permute-start.4 = (bf16[768,1024]{1,0:T(8,128)(2,1)}, bf16[768,1024]{1,0:T(8,128)(2,1)}, u32[]{:S(2)}, u32[]{:S(2)}) collective-permute-start(bf16[768,1024]{1,0:T(8,128)(2,1)} %xs.1), channel_id=1, source_target_pairs={{0,12},{1,13},{2,6},{3,7},{4,0},{5,1},{6,10},{7,11},{8,4},{9,5},{1... | collective-permute-start | bytes 4718600 | tf_op jit(solution)/shard_map/ppermute | solution.py:56
  7.6 6.7 %cut.2 = (bf16[784,640]{1,0:T(8,128)(2,1)}, bf16[784,640]{1,0:T(8,128)(2,1)}, bf16[784,640]{1,0:T(8,128)(2,1)}, bf16[784,640]{1,0:T(8,128)(2,1)}) custom-call(s32[2]{0:T(128)} %pad_add_fusion.places, bf16[16,128]{1,0:T(8,128)(2,1)} %broadcast_in_dim.2.info.own_info, bf16[768,5120]{1,0:T(8,128)(2,1)} %refs_0_.3, bf16[768,5120]{1,0:T(8,128)(2,1)} %refs_0_.3), custom_call_target="tpu_custom_call" | custom-call | flops 1 | bytes 1 | tf_op jit(solution)/shard_map/cut/pallas_call | solution.py:96
  14.3 1.7 %collective-permute-start.6 = (bf16[784,640]{1,0:T(8,128)(2,1)}, bf16[784,640]{1,0:T(8,128)(2,1)}, u32[]{:S(2)}, u32[]{:S(2)}) collective-permute-start(bf16[784,640]{1,0:T(8,128)(2,1)} %get-tuple-element.53), channel_id=1, source_target_pairs={{0,12},{1,13},{2,6},{3,7},{4,0},{5,1},{6,10},{7,11},{8,4},{9,5},{1... | collective-permute-start | bytes 3010568 | tf_op jit(solution)/shard_map/ppermute | solution.py:56
  16.9 6.7 %cut.3 = (bf16[784,640]{1,0:T(8,128)(2,1)}, bf16[784,640]{1,0:T(8,128)(2,1)}, bf16[784,640]{1,0:T(8,128)(2,1)}, bf16[784,640]{1,0:T(8,128)(2,1)}) custom-call(s32[2]{0:T(128)} %pad_add_fusion.1.places, bf16[16,128]{1,0:T(8,128)(2,1)} %broadcast_in_dim.2.info.own_info, bf16[768,5120]{1,0:T(8,128)(2,1)} %refs_0_.3, bf16[768,5120]{1,0:T(8,128)(2,1)} %refs_0_.3), custom_call_target="tpu_custom_call" | custom-call | flops 1 | bytes 1 | tf_op jit(solution)/shard_map/cut/pallas_call | solution.py:96
  23.6 7.8 %half.1 = bf16[784,3584]{1,0:T(8,128)(2,1)} custom-call(s32[1]{0:T(128)} %bitcast.12.place, bf16[16,128]{1,0:T(8,128)(2,1)} %broadcast_in_dim.2.info.own_info, bf16[768,5120]{1,0:T(8,128)(2,1)} %refs_0_.3, bf16[768,1024]{1,0:T(8,128)(2,1)} %xs.1), custom_call_target="tpu_custom_call" | custom-call | flops 1 | bytes 1 | tf_op jit(solution)/shard_map/half/pallas_call | solution.py:131
  31.5 9.6 %conditional.2 = (bf16[784,3584]{1,0:T(8,128)(2,1)}) conditional(s32[]{:T(128)} %bitcast.11, () %tuple.26, bf16[784,3584]{1,0:T(8,128)(2,1)} %half.1), branch_computations={%region_0.1_spmd, %region_1.2_spmd} | conditional | bytes 22478896 | solution.py:484
  31.6 9.5 %collective-permute-done = bf16[784,3584]{1,0:T(8,128)(2,1)} collective-permute-done((bf16[784,3584]{1,0:T(8,128)(2,1)}, bf16[784,3584]{1,0:T(8,128)(2,1)}, u32[]{:S(2)}, u32[]{:S(2)}) %collective-permute-start) | collective-permute-done | bytes 5619744 | tf_op jit(solution)/shard_map/cond/branch_1_fun/ppermute | solution.py:56
  41.1 1.7 %collective-permute-start.7 = (bf16[784,640]{1,0:T(8,128)(2,1)}, bf16[784,640]{1,0:T(8,128)(2,1)}, u32[]{:S(2)}, u32[]{:S(2)}) collective-permute-start(bf16[784,640]{1,0:T(8,128)(2,1)} %get-tuple-element.56), channel_id=1, source_target_pairs={{0,2},{1,3},{2,0},{3,1},{4,6},{5,7},{6,4},{7,5},{8,10},{9,11},{10,... | collective-permute-start | bytes 3010568 | tf_op jit(solution)/shard_map/ppermute | solution.py:56
  42.9 6.0 %conditional.3 = (bf16[768,1024]{1,0:T(8,128)(2,1)}, bf16[768,1024]{1,0:T(8,128)(2,1)}) conditional(s32[]{:T(128)} %bitcast.11, () %tuple.28, (bf16[768,1024]{1,0:T(8,128)(2,1)}, bf16[768,1024]{1,0:T(8,128)(2,1)}) %tuple.29), branch_computations={%region_2.3_spmd, %region_3.4_spmd} | conditional | bytes 12583008 | solution.py:484
  43.4 3.2 %collective-permute-done.1 = bf16[768,1024]{1,0:T(8,128)(2,1)} collective-permute-done((bf16[768,1024]{1,0:T(8,128)(2,1)}, bf16[768,1024]{1,0:T(8,128)(2,1)}, u32[]{:S(2)}, u32[]{:S(2)}) %collective-permute-start.1) | collective-permute-done | bytes 1572896 | tf_op jit(solution)/shard_map/cond/branch_1_fun/ppermute | solution.py:56
  46.7 2.2 %collective-permute-done.2 = bf16[768,1024]{1,0:T(8,128)(2,1)} collective-permute-done((bf16[768,1024]{1,0:T(8,128)(2,1)}, bf16[768,1024]{1,0:T(8,128)(2,1)}, u32[]{:S(2)}, u32[]{:S(2)}) %collective-permute-start.2) | collective-permute-done | bytes 1572896 | tf_op jit(solution)/shard_map/cond/branch_1_fun/ppermute | solution.py:56
  48.9 3.8 %collective-permute-start.8 = (bf16[784,640]{1,0:T(8,128)(2,1)}, bf16[784,640]{1,0:T(8,128)(2,1)}, u32[]{:S(2)}, u32[]{:S(2)}) collective-permute-start(bf16[784,640]{1,0:T(8,128)(2,1)} %get-tuple-element.57), channel_id=1, source_target_pairs={{0,12},{1,13},{2,6},{3,7},{4,0},{5,1},{6,10},{7,11},{8,4},{9,5},{1... | collective-permute-start | bytes 3010568 | tf_op jit(solution)/shard_map/ppermute | solution.py:56
  53.4 8.3 %collective-permute-done.6.zs_one.refs_4_ = bf16[784,640]{1,0:T(8,128)(2,1)} collective-permute-done((bf16[784,640]{1,0:T(8,128)(2,1)}, bf16[784,640]{1,0:T(8,128)(2,1)}, u32[]{:S(2)}, u32[]{:S(2)}) %collective-permute-start.6) | collective-permute-done | bytes 1003552 | tf_op jit(solution)/shard_map/ppermute | solution.py:56
  61.7 1.7 %collective-permute-start.10 = (bf16[784,640]{1,0:T(8,128)(2,1)}, bf16[784,640]{1,0:T(8,128)(2,1)}, u32[]{:S(2)}, u32[]{:S(2)}) collective-permute-start(bf16[784,640]{1,0:T(8,128)(2,1)} %get-tuple-element.64), channel_id=1, source_target_pairs={{0,13},{1,12},{2,7},{3,6},{4,1},{5,0},{6,11},{7,10},{8,5},{9,4},{1... | collective-permute-start | bytes 3010568 | tf_op jit(solution)/shard_map/ppermute | solution.py:56
  64.2 18.4 %grams.1.gram.refs_6_ = f32[7,768,768]{2,1,0:T(8,128)} custom-call(s32[6]{0:T(128)} %stack.48.flags, bf16[768,1024]{1,0:T(8,128)(2,1)} %xs.1, bf16[784,3584]{1,0:T(8,128)(2,1)} %get-tuple-element.79.xc.x_half.refs_1_, bf16[768,1024]{1,0:T(8,128)(2,1)} %collective-permute-done.3.ys, bf16[768,1024]{1,0:T(8,128)(2,1)} %get-tuple-element.59.yc, ...), custom_call_target="tpu_custom_call" | custom-call | flops 1 | bytes 1 | tf_op jit(solution)/shard_map/grams/pallas_call | solution.py:195
  82.6 3.1 %collective-permute-done.7.ys_two.refs_2_ = bf16[784,640]{1,0:T(8,128)(2,1)} collective-permute-done((bf16[784,640]{1,0:T(8,128)(2,1)}, bf16[784,640]{1,0:T(8,128)(2,1)}, u32[]{:S(2)}, u32[]{:S(2)}) %collective-permute-start.7) | collective-permute-done | bytes 1003552 | tf_op jit(solution)/shard_map/ppermute | solution.py:56
  85.7 17.5 %first.1 = (f32[6,48,128]{2,1,0:T(8,128)}, bf16[6,16,128]{2,1,0:T(8,128)(2,1)}) custom-call(s32[6]{0:T(128)} %stack.48.flags, bf16[16,128]{1,0:T(8,128)(2,1)} %broadcast_in_dim.2.info.own_info, bf16[768,5120]{1,0:T(8,128)(2,1)} %refs_0_.3, bf16[784,3584]{1,0:T(8,128)(2,1)} %get-tuple-element.79.xc.x_half.refs_1_, ...), custom_call_target="tpu_custom_call" | custom-call | flops 1 | bytes 1 | tf_op jit(solution)/shard_map/first/pallas_call | solution.py:514
  103.2 1.4 %collective-permute-done.10.refs_5_ = bf16[784,640]{1,0:T(8,128)(2,1)} collective-permute-done((bf16[784,640]{1,0:T(8,128)(2,1)}, bf16[784,640]{1,0:T(8,128)(2,1)}, u32[]{:S(2)}, u32[]{:S(2)}) %collective-permute-start.10) | collective-permute-done | bytes 1003552 | tf_op jit(solution)/shard_map/ppermute | solution.py:56
  106.4 7.9 %later.2 = (f32[6,48,128]{2,1,0:T(8,128)S(1)}, bf16[6,16,128]{2,1,0:T(8,128)(2,1)S(1)}) custom-call(bf16[6,16,128]{2,1,0:T(8,128)(2,1)S(1)} %copy-done.1, f32[6,48,128]{2,1,0:T(8,128)S(1)} %copy-done, bf16[768,5120]{1,0:T(8,128)(2,1)} %refs_0_.3, bf16[784,3584]{1,0:T(8,128)(2,1)} %get-tuple-element.79.xc.x_half.refs_1_, ...), custom_call_target="tpu_custom_call" | custom-call | flops 1 | bytes 1 | tf_op jit(solution)/shard_map/later/pallas_call | solution.py:529
  114.2 11.5 %collective-permute-done.11.refs_3_ = bf16[784,640]{1,0:T(8,128)(2,1)} collective-permute-done((bf16[784,640]{1,0:T(8,128)(2,1)}, bf16[784,640]{1,0:T(8,128)(2,1)}, u32[]{:S(2)}, u32[]{:S(2)}) %collective-permute-start.11) | collective-permute-done | bytes 1003552 | tf_op jit(solution)/shard_map/ppermute | solution.py:56
  125.8 7.9 %later.3 = (f32[48,96]{1,0:T(8,128)S(1)}, f32[48,96]{1,0:T(8,128)S(1)}, f32[48,96]{1,0:T(8,128)S(1)}, f32[48,96]{1,0:T(8,128)S(1)}, f32[48,96]{1,0:T(8,128)S(1)}, /*index=5*/f32[48,96]{1,0:T(8,128)S(1)}) custom-call(bf16[6,16,128]{2,1,0:T(8,128)(2,1)S(1)} %get-tuple-element.65.notes, f32[6,48,128]{2,1,0:T(8,128)S(1)} %get-tuple-element.66.earlier, ...), custom_call_target="tpu_custom_call" | custom-call | flops 1 | bytes 1 | tf_op jit(solution)/shard_map/later/pallas_call | solution.py:529
  133.6 2.6 %collective-permute-start.13 = (f32[48,96]{1,0:T(8,128)S(1)}, f32[48,96]{1,0:T(8,128)S(1)}, u32[]{:S(2)}, u32[]{:S(2)}) collective-permute-start(f32[48,96]{1,0:T(8,128)S(1)} %get-tuple-element.70), channel_id=1, source_target_pairs={{0,1},{1,0},{2,3},{3,2},{4,5},{5,4},{6,7},{7,6},{8,9},{9,8},{10,11... | collective-permute-start | bytes 55304 | tf_op jit(solution)/shard_map/ppermute | solution.py:56
  136.3 1.4 collective-permute-start.15
  140.1 3.5 %collective-permute-done.16 = f32[48,96]{1,0:T(8,128)S(1)} collective-permute-done((f32[48,96]{1,0:T(8,128)S(1)}, f32[48,96]{1,0:T(8,128)S(1)}, u32[]{:S(2)}, u32[]{:S(2)}) %collective-permute-start.16) | collective-permute-done | bytes 18464 | tf_op jit(solution)/shard_map/ppermute | solution.py:56
  (36 shorter events, 10.2 us)
Async XLA Ops:
  0.0 42.9 %collective-permute-start.4 = (bf16[768,1024]{1,0:T(8,128)(2,1)}, bf16[768,1024]{1,0:T(8,128)(2,1)}, u32[]{:S(2)}, u32[]{:S(2)}) collective-permute-start(bf16[768,1024]{1,0:T(8,128)(2,1)} %xs.1), channel_id=1, source_target_pairs={{0,12},{1,13},{2,6},{3,7},{4,0},{5,1},{6,10},{7,11},{8,4},{9,5},{1... | collective-permute-start | bytes 4718600 | tf_op jit(solution)/shard_map/ppermute | solution.py:56
  5.0 37.8 %collective-permute-start.3 = (bf16[768,1024]{1,0:T(8,128)(2,1)}, bf16[768,1024]{1,0:T(8,128)(2,1)}, u32[]{:S(2)}, u32[]{:S(2)}) collective-permute-start(bf16[768,1024]{1,0:T(8,128)(2,1)} %xs.1), channel_id=1, source_target_pairs={{0,2},{1,3},{2,0},{3,1},{4,6},{5,7},{6,4},{7,5},{8,10},{9,11},{10,... | collective-permute-start | bytes 4718600 | tf_op jit(solution)/shard_map/ppermute | solution.py:56
  14.3 47.4 %collective-permute-start.6 = (bf16[784,640]{1,0:T(8,128)(2,1)}, bf16[784,640]{1,0:T(8,128)(2,1)}, u32[]{:S(2)}, u32[]{:S(2)}) collective-permute-start(bf16[784,640]{1,0:T(8,128)(2,1)} %get-tuple-element.53), channel_id=1, source_target_pairs={{0,12},{1,13},{2,6},{3,7},{4,0},{5,1},{6,10},{7,11},{8,4},{9,5},{1... | collective-permute-start | bytes 3010568 | tf_op jit(solution)/shard_map/ppermute | solution.py:56
  16.1 48.1 %collective-permute-start.5 = (bf16[784,640]{1,0:T(8,128)(2,1)}, bf16[784,640]{1,0:T(8,128)(2,1)}, u32[]{:S(2)}, u32[]{:S(2)}) collective-permute-start(bf16[784,640]{1,0:T(8,128)(2,1)} %get-tuple-element.45), channel_id=1, source_target_pairs={{0,2},{1,3},{2,0},{3,1},{4,6},{5,7},{6,4},{7,5},{8,10},{9,11},{10,... | collective-permute-start | bytes 3010568 | tf_op jit(solution)/shard_map/ppermute | solution.py:56
  23.6 7.8 %copy-start.2 = (s32[1,2]{1,0:T(1,128)S(1)}, s32[1,2]{1,0:T(1,128)}, u32[]{:S(2)}) copy-start(s32[1,2]{1,0:T(1,128)} %param.11) | copy-start | bytes 28
  31.5 9.6 %collective-permute-start = (bf16[784,3584]{1,0:T(8,128)(2,1)}, bf16[784,3584]{1,0:T(8,128)(2,1)}, u32[]{:S(2)}, u32[]{:S(2)}) collective-permute-start(bf16[784,3584]{1,0:T(8,128)(2,1)} %param.1), channel_id=1, source_target_pairs={{0,1},{1,0},{2,3},{3,2},{4,5},{5,4},{6,7},{7,6},{8,9},{9,8},{10,11... | collective-permute-start | bytes 16859144 | tf_op jit(solution)/shard_map/cond/branch_1_fun/ppermute | solution.py:56
  41.1 44.5 %collective-permute-start.7 = (bf16[784,640]{1,0:T(8,128)(2,1)}, bf16[784,640]{1,0:T(8,128)(2,1)}, u32[]{:S(2)}, u32[]{:S(2)}) collective-permute-start(bf16[784,640]{1,0:T(8,128)(2,1)} %get-tuple-element.56), channel_id=1, source_target_pairs={{0,2},{1,3},{2,0},{3,1},{4,6},{5,7},{6,4},{7,5},{8,10},{9,11},{10,... | collective-permute-start | bytes 3010568 | tf_op jit(solution)/shard_map/ppermute | solution.py:56
  42.9 3.8 %collective-permute-start.1 = (bf16[768,1024]{1,0:T(8,128)(2,1)}, bf16[768,1024]{1,0:T(8,128)(2,1)}, u32[]{:S(2)}, u32[]{:S(2)}) collective-permute-start(bf16[768,1024]{1,0:T(8,128)(2,1)} %get-tuple-element.13), channel_id=1, source_target_pairs={{0,1},{1,0},{2,3},{3,2},{4,5},{5,4},{6,7},{7,6},{8,9},{9,8},{10,11... | collective-permute-start | bytes 4718600 | tf_op jit(solution)/shard_map/cond/branch_1_fun/ppermute | solution.py:56
  42.9 6.0 %collective-permute-start.2 = (bf16[768,1024]{1,0:T(8,128)(2,1)}, bf16[768,1024]{1,0:T(8,128)(2,1)}, u32[]{:S(2)}, u32[]{:S(2)}) collective-permute-start(bf16[768,1024]{1,0:T(8,128)(2,1)} %get-tuple-element.14), channel_id=1, source_target_pairs={{0,1},{1,0},{2,3},{3,2},{4,5},{5,4},{6,7},{7,6},{8,9},{9,8},{10,11... | collective-permute-start | bytes 4718600 | tf_op jit(solution)/shard_map/cond/branch_1_fun/ppermute | solution.py:56
  48.9 55.8 %collective-permute-start.9 = (bf16[784,640]{1,0:T(8,128)(2,1)}, bf16[784,640]{1,0:T(8,128)(2,1)}, u32[]{:S(2)}, u32[]{:S(2)}) collective-permute-start(bf16[784,640]{1,0:T(8,128)(2,1)} %get-tuple-element.47), channel_id=1, source_target_pairs={{0,3},{1,2},{2,1},{3,0},{4,7},{5,6},{6,5},{7,4},{8,11},{9,10},{10,... | collective-permute-start | bytes 3010568 | tf_op jit(solution)/shard_map/ppermute | solution.py:56
  48.9 36.8 %collective-permute-start.8 = (bf16[784,640]{1,0:T(8,128)(2,1)}, bf16[784,640]{1,0:T(8,128)(2,1)}, u32[]{:S(2)}, u32[]{:S(2)}) collective-permute-start(bf16[784,640]{1,0:T(8,128)(2,1)} %get-tuple-element.57), channel_id=1, source_target_pairs={{0,12},{1,13},{2,6},{3,7},{4,0},{5,1},{6,10},{7,11},{8,4},{9,5},{1... | collective-permute-start | bytes 3010568 | tf_op jit(solution)/shard_map/ppermute | solution.py:56
  61.7 43.0 %collective-permute-start.10 = (bf16[784,640]{1,0:T(8,128)(2,1)}, bf16[784,640]{1,0:T(8,128)(2,1)}, u32[]{:S(2)}, u32[]{:S(2)}) collective-permute-start(bf16[784,640]{1,0:T(8,128)(2,1)} %get-tuple-element.64), channel_id=1, source_target_pairs={{0,13},{1,12},{2,7},{3,6},{4,1},{5,0},{6,11},{7,10},{8,5},{9,4},{1... | collective-permute-start | bytes 3010568 | tf_op jit(solution)/shard_map/ppermute | solution.py:56
  64.2 61.6 %collective-permute-start.11 = (bf16[784,640]{1,0:T(8,128)(2,1)}, bf16[784,640]{1,0:T(8,128)(2,1)}, u32[]{:S(2)}, u32[]{:S(2)}) collective-permute-start(bf16[784,640]{1,0:T(8,128)(2,1)} %get-tuple-element.67), channel_id=1, source_target_pairs={{0,3},{1,2},{2,1},{3,0},{4,7},{5,6},{6,5},{7,4},{8,11},{9,10},{10,... | collective-permute-start | bytes 3010568 | tf_op jit(solution)/shard_map/ppermute | solution.py:56
  85.7 40.1 %collective-permute-start.12 = (bf16[784,640]{1,0:T(8,128)(2,1)}, bf16[784,640]{1,0:T(8,128)(2,1)}, u32[]{:S(2)}, u32[]{:S(2)}) collective-permute-start(bf16[784,640]{1,0:T(8,128)(2,1)} %get-tuple-element.68), channel_id=1, source_target_pairs={{0,13},{1,12},{2,7},{3,6},{4,1},{5,0},{6,11},{7,10},{8,5},{9,4},{1... | collective-permute-start | bytes 3010568 | tf_op jit(solution)/shard_map/ppermute | solution.py:56
  104.7 0.9 copy-start
  105.6 0.7 copy-start.1
  133.6 5.0 %collective-permute-start.13 = (f32[48,96]{1,0:T(8,128)S(1)}, f32[48,96]{1,0:T(8,128)S(1)}, u32[]{:S(2)}, u32[]{:S(2)}) collective-permute-start(f32[48,96]{1,0:T(8,128)S(1)} %get-tuple-element.70), channel_id=1, source_target_pairs={{0,1},{1,0},{2,3},{3,2},{4,5},{5,4},{6,7},{7,6},{8,9},{9,8},{10,11... | collective-permute-start | bytes 55304 | tf_op jit(solution)/shard_map/ppermute | solution.py:56
  136.3 3.8 %collective-permute-start.14 = (f32[48,96]{1,0:T(8,128)S(1)}, f32[48,96]{1,0:T(8,128)S(1)}, u32[]{:S(2)}, u32[]{:S(2)}) collective-permute-start(f32[48,96]{1,0:T(8,128)S(1)} %get-tuple-element.71), channel_id=1, source_target_pairs={{0,2},{1,3},{2,0},{3,1},{4,6},{5,7},{6,4},{7,5},{8,10},{9,11},{10,... | collective-permute-start | bytes 55304 | tf_op jit(solution)/shard_map/ppermute | solution.py:56
  136.3 3.8 %collective-permute-start.15 = (f32[48,96]{1,0:T(8,128)S(1)}, f32[48,96]{1,0:T(8,128)S(1)}, u32[]{:S(2)}, u32[]{:S(2)}) collective-permute-start(f32[48,96]{1,0:T(8,128)S(1)} %get-tuple-element.72), channel_id=1, source_target_pairs={{0,3},{1,2},{2,1},{3,0},{4,7},{5,6},{6,5},{7,4},{8,11},{9,10},{10,... | collective-permute-start | bytes 55304 | tf_op jit(solution)/shard_map/ppermute | solution.py:56
  137.7 5.9 %collective-permute-start.16 = (f32[48,96]{1,0:T(8,128)S(1)}, f32[48,96]{1,0:T(8,128)S(1)}, u32[]{:S(2)}, u32[]{:S(2)}) collective-permute-start(f32[48,96]{1,0:T(8,128)S(1)} %get-tuple-element.73), channel_id=1, source_target_pairs={{0,4},{1,5},{2,14},{3,15},{4,8},{5,9},{6,2},{7,3},{8,12},{9,13},{1... | collective-permute-start | bytes 55304 | tf_op jit(solution)/shard_map/ppermute | solution.py:56
  137.7 5.9 %collective-permute-start.17 = (f32[48,96]{1,0:T(8,128)S(1)}, f32[48,96]{1,0:T(8,128)S(1)}, u32[]{:S(2)}, u32[]{:S(2)}) collective-permute-start(f32[48,96]{1,0:T(8,128)S(1)} %get-tuple-element.74), channel_id=1, source_target_pairs={{0,5},{1,4},{2,15},{3,14},{4,9},{5,8},{6,3},{7,2},{8,13},{9,12},{1... | collective-permute-start | bytes 55304 | tf_op jit(solution)/shard_map/ppermute | solution.py:56
where the time goes:
time: 145 us; the launch traced here: 144 us
  Pallas kernels  72.9 us (50%)
  waiting for transfers between devices  45.2 us (31%)
  starting transfers between devices  20 us (14%)
  other arithmetic  3.17 us (2%)
  local copies, waits for them, and re-layouts  2.88 us (2%)
    ppermute x18, waiting for transfers between devices, send(): return lax.ppermute(value, 'ex', pairs)  45.2 us
    ppermute x18, starting transfers between devices, send(): return lax.ppermute(value, 'ex', pairs)  20 us
    pallas_call x1, Pallas kernels, grams(): pl.pallas_call(grams_kernel, in_specs=[pl.BlockSpec(memory_space=pltpu.SM...  18.4 us
    pallas_call x1, Pallas kernels, per_device(): pl.pallas_call(functools.partial(first_kernel, factor), in_specs=[smem, v...  17.5 us
    pallas_call x2, Pallas kernels, later(): pl.pallas_call(functools.partial(later_kernel, factor, at), in_specs=[hbm...  15.7 us
    pallas_call x2, Pallas kernels, cut(): pl.pallas_call(cut_kernel, grid_spec=pltpu.PrefetchScalarGridSpec(num_sca...  13.4 us
    pallas_call x1, Pallas kernels, cut_half(): pl.pallas_call(functools.partial(half_kernel, steps), grid_spec=pltpu.Pre...  7.84 us
  transfers between devices with their start and end apart: 18, of which 10 were waited for; matrix products, arithmetic and copies ran while one was open for 3% of the time, Pallas kernels for 45%

commit v1 on v0

--- a/solution.py
+++ b/solution.py
@@ -299,21 +299,32 @@
     return total
 
 
-def copies_of(loads, sems):
-    return {
-        key: pltpu.make_async_copy(source, target, sems.at[at])
-        for at, (key, (source, target)) in enumerate(loads.items())
-    }
+def copies_of(loads, sems, step=None):
+    copies = {}
+    for at, (key, (source, target)) in enumerate(loads.items()):
+        rows = target.shape[0]
+        pieces = [
+            (first, min(step or rows, rows - first)) for first in range(0, rows, step or rows)
+        ]
+        copies[key] = [
+            pltpu.make_async_copy(
+                source.at[pl.ds(first, size)], target.at[pl.ds(first, size)], sems.at[at, piece]
+            )
+            for piece, (first, size) in enumerate(pieces)
+        ]
+    return copies
 
 
 def start(copies, *keys):
     for key in keys:
-        copies[key].start()
+        for copy in copies[key]:
+            copy.start()
 
 
 def wait(copies, *keys):
     for key in keys:
-        copies[key].wait()
+        for copy in copies[key]:
+            copy.wait()
 
 
 def info_row(notes, block):
@@ -400,7 +411,7 @@
         "g2": (gram.at[2], gram_v.at[3]),
         "notes": (notes, notes_v),
         "earlier": (earlier, earlier_v),
-    }, sems)
+    }, sems, 192)
     start(copies, YC, XC, ZC)
     wait(copies, YC, XC)
     start(copies, "g4", YS, ZS)
@@ -519,7 +530,7 @@
         scratch_shapes=[own_v] + [slice_v] * 3 + [
             pltpu.VMEM((rows, 2 * quarter), acts.dtype),
             pltpu.VMEM((rows + INFO, 2 * quarter), acts.dtype),
-        ] + shared + [pltpu.SemaphoreType.DMA((12,))],
+        ] + shared + [pltpu.SemaphoreType.DMA((12, 1))],
         compiler_params=params,
         cost_estimate=SMALL,
         name="first",
@@ -535,7 +546,7 @@
                 pltpu.VMEM((6, rows + INFO, messages[0].shape[1]), acts.dtype),
                 pltpu.VMEM(all_notes.shape, acts.dtype),
                 pltpu.VMEM(partial_sums.shape, jnp.float32),
-            ] + shared + [pltpu.SemaphoreType.DMA((12,))],
+            ] + shared + [pltpu.SemaphoreType.DMA((12, 5))],
             compiler_params=pltpu.CompilerParams(vmem_limit_bytes=LATER_VMEM_BYTES),
             cost_estimate=SMALL,
             name="later",
@@ -551,11 +562,11 @@
     )
 
     total = sums[XS]
-    total = total + send(sums[XC], stay, 1)
+    total = total + send(sums[ZS], against, 0)
+    total = total + send(sums[ZC], against, 1)
     total = total + send(sums[YS], across, 0)
     total = total + send(sums[YC], across, 1)
-    total = total + send(sums[ZS], against, 0)
-    total = total + send(sums[ZC], against, 1)
+    total = total + send(sums[XC], stay, 1)
     return total.T
 
 

time: 145 us -> 143 us (0.986)
  waiting for transfers between devices: 45.2 us -> 42.3 us
    ppermute x18, waiting for transfers between devices: 45.2 us -> 42.3 us  [send(): return lax.ppermute(value, 'ex', pairs)]
  transfers between devices with their start and end apart: 18 -> 18, of which waited for: 10 -> 10; matrix products, arithmetic and copies ran while one was open for 3% -> 3% of each run, Pallas kernels for 45% -> 46%
where the time goes in v1:
time: 143 us; the launch traced here: 142 us
  Pallas kernels  73.8 us (52%)
  waiting for transfers between devices  42.3 us (30%)
  starting transfers between devices  20 us (14%)
  other arithmetic  3.17 us (2%)
  local copies, waits for them, and re-layouts  2.88 us (2%)
    ppermute x18, waiting for transfers between devices, send(): return lax.ppermute(value, 'ex', pairs)  42.3 us
    ppermute x18, starting transfers between devices, send(): return lax.ppermute(value, 'ex', pairs)  20 us
    pallas_call x1, Pallas kernels, grams(): pl.pallas_call(grams_kernel, in_specs=[pl.BlockSpec(memory_space=pltpu.SM...  18.4 us
    pallas_call x1, Pallas kernels, per_device(): pl.pallas_call(functools.partial(first_kernel, factor), in_specs=[smem, v...  17.5 us
    pallas_call x2, Pallas kernels, later(): pl.pallas_call(functools.partial(later_kernel, factor, at), in_specs=[hbm...  16.6 us
    pallas_call x2, Pallas kernels, cut(): pl.pallas_call(cut_kernel, grid_spec=pltpu.PrefetchScalarGridSpec(num_sca...  13.4 us
    pallas_call x1, Pallas kernels, cut_half(): pl.pallas_call(functools.partial(half_kernel, steps), grid_spec=pltpu.Pre...  7.84 us
  transfers between devices with their start and end apart: 18, of which 10 were waited for; matrix products, arithmetic and copies ran while one was open for 3% of the time, Pallas kernels for 46%

profile of v1, /device:TPU:0, one launch (start us, length us, event | category | flops | bytes accessed | tf_op | source)
XLA Modules:
  0.0 142.3 jit_solution(11079501456996036814)
XLA Ops:
  0.0 5.0 %collective-permute-start.4 = (bf16[768,1024]{1,0:T(8,128)(2,1)}, bf16[768,1024]{1,0:T(8,128)(2,1)}, u32[]{:S(2)}, u32[]{:S(2)}) collective-permute-start(bf16[768,1024]{1,0:T(8,128)(2,1)} %xs.1), channel_id=1, source_target_pairs={{0,12},{1,13},{2,6},{3,7},{4,0},{5,1},{6,10},{7,11},{8,4},{9,5},{1... | collective-permute-start | bytes 4718600 | tf_op jit(solution)/shard_map/ppermute | solution.py:56
  7.6 6.7 %cut.2 = (bf16[784,640]{1,0:T(8,128)(2,1)}, bf16[784,640]{1,0:T(8,128)(2,1)}, bf16[784,640]{1,0:T(8,128)(2,1)}, bf16[784,640]{1,0:T(8,128)(2,1)}) custom-call(s32[2]{0:T(128)} %pad_add_fusion.places, bf16[16,128]{1,0:T(8,128)(2,1)} %broadcast_in_dim.2.info.own_info, bf16[768,5120]{1,0:T(8,128)(2,1)} %refs_0_.3, bf16[768,5120]{1,0:T(8,128)(2,1)} %refs_0_.3), custom_call_target="tpu_custom_call" | custom-call | flops 1 | bytes 1 | tf_op jit(solution)/shard_map/cut/pallas_call | solution.py:96
  14.3 1.7 %collective-permute-start.6 = (bf16[784,640]{1,0:T(8,128)(2,1)}, bf16[784,640]{1,0:T(8,128)(2,1)}, u32[]{:S(2)}, u32[]{:S(2)}) collective-permute-start(bf16[784,640]{1,0:T(8,128)(2,1)} %get-tuple-element.53), channel_id=1, source_target_pairs={{0,12},{1,13},{2,6},{3,7},{4,0},{5,1},{6,10},{7,11},{8,4},{9,5},{1... | collective-permute-start | bytes 3010568 | tf_op jit(solution)/shard_map/ppermute | solution.py:56
  16.9 6.7 %cut.3 = (bf16[784,640]{1,0:T(8,128)(2,1)}, bf16[784,640]{1,0:T(8,128)(2,1)}, bf16[784,640]{1,0:T(8,128)(2,1)}, bf16[784,640]{1,0:T(8,128)(2,1)}) custom-call(s32[2]{0:T(128)} %pad_add_fusion.1.places, bf16[16,128]{1,0:T(8,128)(2,1)} %broadcast_in_dim.2.info.own_info, bf16[768,5120]{1,0:T(8,128)(2,1)} %refs_0_.3, bf16[768,5120]{1,0:T(8,128)(2,1)} %refs_0_.3), custom_call_target="tpu_custom_call" | custom-call | flops 1 | bytes 1 | tf_op jit(solution)/shard_map/cut/pallas_call | solution.py:96
  23.6 7.8 %half.1 = bf16[784,3584]{1,0:T(8,128)(2,1)} custom-call(s32[1]{0:T(128)} %bitcast.12.place, bf16[16,128]{1,0:T(8,128)(2,1)} %broadcast_in_dim.2.info.own_info, bf16[768,5120]{1,0:T(8,128)(2,1)} %refs_0_.3, bf16[768,1024]{1,0:T(8,128)(2,1)} %xs.1), custom_call_target="tpu_custom_call" | custom-call | flops 1 | bytes 1 | tf_op jit(solution)/shard_map/half/pallas_call | solution.py:131
  31.5 9.6 %conditional.2 = (bf16[784,3584]{1,0:T(8,128)(2,1)}) conditional(s32[]{:T(128)} %bitcast.11, () %tuple.26, bf16[784,3584]{1,0:T(8,128)(2,1)} %half.1), branch_computations={%region_0.1_spmd, %region_1.2_spmd} | conditional | bytes 22478896 | solution.py:495
  31.6 9.5 %collective-permute-done = bf16[784,3584]{1,0:T(8,128)(2,1)} collective-permute-done((bf16[784,3584]{1,0:T(8,128)(2,1)}, bf16[784,3584]{1,0:T(8,128)(2,1)}, u32[]{:S(2)}, u32[]{:S(2)}) %collective-permute-start) | collective-permute-done | bytes 5619744 | tf_op jit(solution)/shard_map/cond/branch_1_fun/ppermute | solution.py:56
  41.1 1.7 %collective-permute-start.7 = (bf16[784,640]{1,0:T(8,128)(2,1)}, bf16[784,640]{1,0:T(8,128)(2,1)}, u32[]{:S(2)}, u32[]{:S(2)}) collective-permute-start(bf16[784,640]{1,0:T(8,128)(2,1)} %get-tuple-element.56), channel_id=1, source_target_pairs={{0,2},{1,3},{2,0},{3,1},{4,6},{5,7},{6,4},{7,5},{8,10},{9,11},{10,... | collective-permute-start | bytes 3010568 | tf_op jit(solution)/shard_map/ppermute | solution.py:56
  42.9 6.0 %conditional.3 = (bf16[768,1024]{1,0:T(8,128)(2,1)}, bf16[768,1024]{1,0:T(8,128)(2,1)}) conditional(s32[]{:T(128)} %bitcast.11, () %tuple.28, (bf16[768,1024]{1,0:T(8,128)(2,1)}, bf16[768,1024]{1,0:T(8,128)(2,1)}) %tuple.29), branch_computations={%region_2.3_spmd, %region_3.4_spmd} | conditional | bytes 12583008 | solution.py:495
  43.4 3.2 %collective-permute-done.1 = bf16[768,1024]{1,0:T(8,128)(2,1)} collective-permute-done((bf16[768,1024]{1,0:T(8,128)(2,1)}, bf16[768,1024]{1,0:T(8,128)(2,1)}, u32[]{:S(2)}, u32[]{:S(2)}) %collective-permute-start.1) | collective-permute-done | bytes 1572896 | tf_op jit(solution)/shard_map/cond/branch_1_fun/ppermute | solution.py:56
  46.7 2.2 %collective-permute-done.2 = bf16[768,1024]{1,0:T(8,128)(2,1)} collective-permute-done((bf16[768,1024]{1,0:T(8,128)(2,1)}, bf16[768,1024]{1,0:T(8,128)(2,1)}, u32[]{:S(2)}, u32[]{:S(2)}) %collective-permute-start.2) | collective-permute-done | bytes 1572896 | tf_op jit(solution)/shard_map/cond/branch_1_fun/ppermute | solution.py:56
  48.9 3.8 %collective-permute-start.8 = (bf16[784,640]{1,0:T(8,128)(2,1)}, bf16[784,640]{1,0:T(8,128)(2,1)}, u32[]{:S(2)}, u32[]{:S(2)}) collective-permute-start(bf16[784,640]{1,0:T(8,128)(2,1)} %get-tuple-element.57), channel_id=1, source_target_pairs={{0,12},{1,13},{2,6},{3,7},{4,0},{5,1},{6,10},{7,11},{8,4},{9,5},{1... | collective-permute-start | bytes 3010568 | tf_op jit(solution)/shard_map/ppermute | solution.py:56
  53.4 8.3 %collective-permute-done.6.zs_one.refs_4_ = bf16[784,640]{1,0:T(8,128)(2,1)} collective-permute-done((bf16[784,640]{1,0:T(8,128)(2,1)}, bf16[784,640]{1,0:T(8,128)(2,1)}, u32[]{:S(2)}, u32[]{:S(2)}) %collective-permute-start.6) | collective-permute-done | bytes 1003552 | tf_op jit(solution)/shard_map/ppermute | solution.py:56
  61.7 1.7 %collective-permute-start.10 = (bf16[784,640]{1,0:T(8,128)(2,1)}, bf16[784,640]{1,0:T(8,128)(2,1)}, u32[]{:S(2)}, u32[]{:S(2)}) collective-permute-start(bf16[784,640]{1,0:T(8,128)(2,1)} %get-tuple-element.64), channel_id=1, source_target_pairs={{0,13},{1,12},{2,7},{3,6},{4,1},{5,0},{6,11},{7,10},{8,5},{9,4},{1... | collective-permute-start | bytes 3010568 | tf_op jit(solution)/shard_map/ppermute | solution.py:56
  64.2 18.4 %grams.1.gram.refs_6_ = f32[7,768,768]{2,1,0:T(8,128)} custom-call(s32[6]{0:T(128)} %stack.48.flags, bf16[768,1024]{1,0:T(8,128)(2,1)} %xs.1, bf16[784,3584]{1,0:T(8,128)(2,1)} %get-tuple-element.79.xc.x_half.refs_1_, bf16[768,1024]{1,0:T(8,128)(2,1)} %collective-permute-done.3.ys, bf16[768,1024]{1,0:T(8,128)(2,1)} %get-tuple-element.59.yc, ...), custom_call_target="tpu_custom_call" | custom-call | flops 1 | bytes 1 | tf_op jit(solution)/shard_map/grams/pallas_call | solution.py:195
  82.6 3.1 %collective-permute-done.7.ys_two.refs_2_ = bf16[784,640]{1,0:T(8,128)(2,1)} collective-permute-done((bf16[784,640]{1,0:T(8,128)(2,1)}, bf16[784,640]{1,0:T(8,128)(2,1)}, u32[]{:S(2)}, u32[]{:S(2)}) %collective-permute-start.7) | collective-permute-done | bytes 1003552 | tf_op jit(solution)/shard_map/ppermute | solution.py:56
  85.7 17.5 %first.1 = (f32[6,48,128]{2,1,0:T(8,128)}, bf16[6,16,128]{2,1,0:T(8,128)(2,1)}) custom-call(s32[6]{0:T(128)} %stack.48.flags, bf16[16,128]{1,0:T(8,128)(2,1)} %broadcast_in_dim.2.info.own_info, bf16[768,5120]{1,0:T(8,128)(2,1)} %refs_0_.3, bf16[784,3584]{1,0:T(8,128)(2,1)} %get-tuple-element.79.xc.x_half.refs_1_, ...), custom_call_target="tpu_custom_call" | custom-call | flops 1 | bytes 1 | tf_op jit(solution)/shard_map/first/pallas_call | solution.py:525
  103.2 1.4 %collective-permute-done.10.refs_5_ = bf16[784,640]{1,0:T(8,128)(2,1)} collective-permute-done((bf16[784,640]{1,0:T(8,128)(2,1)}, bf16[784,640]{1,0:T(8,128)(2,1)}, u32[]{:S(2)}, u32[]{:S(2)}) %collective-permute-start.10) | collective-permute-done | bytes 1003552 | tf_op jit(solution)/shard_map/ppermute | solution.py:56
  106.4 8.3 %later.2 = (f32[6,48,128]{2,1,0:T(8,128)S(1)}, bf16[6,16,128]{2,1,0:T(8,128)(2,1)S(1)}) custom-call(bf16[6,16,128]{2,1,0:T(8,128)(2,1)S(1)} %copy-done.1, f32[6,48,128]{2,1,0:T(8,128)S(1)} %copy-done, bf16[768,5120]{1,0:T(8,128)(2,1)} %refs_0_.3, bf16[784,3584]{1,0:T(8,128)(2,1)} %get-tuple-element.79.xc.x_half.refs_1_, ...), custom_call_target="tpu_custom_call" | custom-call | flops 1 | bytes 1 | tf_op jit(solution)/shard_map/later/pallas_call | solution.py:540
  114.7 11.1 %collective-permute-done.11.refs_3_ = bf16[784,640]{1,0:T(8,128)(2,1)} collective-permute-done((bf16[784,640]{1,0:T(8,128)(2,1)}, bf16[784,640]{1,0:T(8,128)(2,1)}, u32[]{:S(2)}, u32[]{:S(2)}) %collective-permute-start.11) | collective-permute-done | bytes 1003552 | tf_op jit(solution)/shard_map/ppermute | solution.py:56
  125.8 8.3 %later.3 = (f32[48,96]{1,0:T(8,128)S(1)}, f32[48,96]{1,0:T(8,128)S(1)}, f32[48,96]{1,0:T(8,128)S(1)}, f32[48,96]{1,0:T(8,128)S(1)}, f32[48,96]{1,0:T(8,128)S(1)}, /*index=5*/f32[48,96]{1,0:T(8,128)S(1)}) custom-call(bf16[6,16,128]{2,1,0:T(8,128)(2,1)S(1)} %get-tuple-element.65.notes, f32[6,48,128]{2,1,0:T(8,128)S(1)} %get-tuple-element.66.earlier, ...), custom_call_target="tpu_custom_call" | custom-call | flops 1 | bytes 1 | tf_op jit(solution)/shard_map/later/pallas_call | solution.py:540
  134.2 2.7 %collective-permute-start.14 = (f32[48,96]{1,0:T(8,128)S(1)}, f32[48,96]{1,0:T(8,128)S(1)}, u32[]{:S(2)}, u32[]{:S(2)}) collective-permute-start(f32[48,96]{1,0:T(8,128)S(1)} %get-tuple-element.71), channel_id=1, source_target_pairs={{0,5},{1,4},{2,15},{3,14},{4,9},{5,8},{6,3},{7,2},{8,13},{9,12},{1... | collective-permute-start | bytes 55304 | tf_op jit(solution)/shard_map/ppermute | solution.py:56
  137.0 1.4 collective-permute-start.15
  139.8 1.8 %collective-permute-done.14 = f32[48,96]{1,0:T(8,128)S(1)} collective-permute-done((f32[48,96]{1,0:T(8,128)S(1)}, f32[48,96]{1,0:T(8,128)S(1)}, u32[]{:S(2)}, u32[]{:S(2)}) %collective-permute-start.14) | collective-permute-done | bytes 18464 | tf_op jit(solution)/shard_map/ppermute | solution.py:56
  (36 shorter events, 9.4 us)
Async XLA Ops:
  0.0 42.9 %collective-permute-start.4 = (bf16[768,1024]{1,0:T(8,128)(2,1)}, bf16[768,1024]{1,0:T(8,128)(2,1)}, u32[]{:S(2)}, u32[]{:S(2)}) collective-permute-start(bf16[768,1024]{1,0:T(8,128)(2,1)} %xs.1), channel_id=1, source_target_pairs={{0,12},{1,13},{2,6},{3,7},{4,0},{5,1},{6,10},{7,11},{8,4},{9,5},{1... | collective-permute-start | bytes 4718600 | tf_op jit(solution)/shard_map/ppermute | solution.py:56
  5.0 37.8 %collective-permute-start.3 = (bf16[768,1024]{1,0:T(8,128)(2,1)}, bf16[768,1024]{1,0:T(8,128)(2,1)}, u32[]{:S(2)}, u32[]{:S(2)}) collective-permute-start(bf16[768,1024]{1,0:T(8,128)(2,1)} %xs.1), channel_id=1, source_target_pairs={{0,2},{1,3},{2,0},{3,1},{4,6},{5,7},{6,4},{7,5},{8,10},{9,11},{10,... | collective-permute-start | bytes 4718600 | tf_op jit(solution)/shard_map/ppermute | solution.py:56
  14.3 47.4 %collective-permute-start.6 = (bf16[784,640]{1,0:T(8,128)(2,1)}, bf16[784,640]{1,0:T(8,128)(2,1)}, u32[]{:S(2)}, u32[]{:S(2)}) collective-permute-start(bf16[784,640]{1,0:T(8,128)(2,1)} %get-tuple-element.53), channel_id=1, source_target_pairs={{0,12},{1,13},{2,6},{3,7},{4,0},{5,1},{6,10},{7,11},{8,4},{9,5},{1... | collective-permute-start | bytes 3010568 | tf_op jit(solution)/shard_map/ppermute | solution.py:56
  16.1 48.1 %collective-permute-start.5 = (bf16[784,640]{1,0:T(8,128)(2,1)}, bf16[784,640]{1,0:T(8,128)(2,1)}, u32[]{:S(2)}, u32[]{:S(2)}) collective-permute-start(bf16[784,640]{1,0:T(8,128)(2,1)} %get-tuple-element.45), channel_id=1, source_target_pairs={{0,2},{1,3},{2,0},{3,1},{4,6},{5,7},{6,4},{7,5},{8,10},{9,11},{10,... | collective-permute-start | bytes 3010568 | tf_op jit(solution)/shard_map/ppermute | solution.py:56
  23.6 7.8 %copy-start.2 = (s32[1,2]{1,0:T(1,128)S(1)}, s32[1,2]{1,0:T(1,128)}, u32[]{:S(2)}) copy-start(s32[1,2]{1,0:T(1,128)} %param.11) | copy-start | bytes 28
  31.5 9.6 %collective-permute-start = (bf16[784,3584]{1,0:T(8,128)(2,1)}, bf16[784,3584]{1,0:T(8,128)(2,1)}, u32[]{:S(2)}, u32[]{:S(2)}) collective-permute-start(bf16[784,3584]{1,0:T(8,128)(2,1)} %param.1), channel_id=1, source_target_pairs={{0,1},{1,0},{2,3},{3,2},{4,5},{5,4},{6,7},{7,6},{8,9},{9,8},{10,11... | collective-permute-start | bytes 16859144 | tf_op jit(solution)/shard_map/cond/branch_1_fun/ppermute | solution.py:56
  41.1 44.5 %collective-permute-start.7 = (bf16[784,640]{1,0:T(8,128)(2,1)}, bf16[784,640]{1,0:T(8,128)(2,1)}, u32[]{:S(2)}, u32[]{:S(2)}) collective-permute-start(bf16[784,640]{1,0:T(8,128)(2,1)} %get-tuple-element.56), channel_id=1, source_target_pairs={{0,2},{1,3},{2,0},{3,1},{4,6},{5,7},{6,4},{7,5},{8,10},{9,11},{10,... | collective-permute-start | bytes 3010568 | tf_op jit(solution)/shard_map/ppermute | solution.py:56
  42.9 3.8 %collective-permute-start.1 = (bf16[768,1024]{1,0:T(8,128)(2,1)}, bf16[768,1024]{1,0:T(8,128)(2,1)}, u32[]{:S(2)}, u32[]{:S(2)}) collective-permute-start(bf16[768,1024]{1,0:T(8,128)(2,1)} %get-tuple-element.13), channel_id=1, source_target_pairs={{0,1},{1,0},{2,3},{3,2},{4,5},{5,4},{6,7},{7,6},{8,9},{9,8},{10,11... | collective-permute-start | bytes 4718600 | tf_op jit(solution)/shard_map/cond/branch_1_fun/ppermute | solution.py:56
  42.9 6.0 %collective-permute-start.2 = (bf16[768,1024]{1,0:T(8,128)(2,1)}, bf16[768,1024]{1,0:T(8,128)(2,1)}, u32[]{:S(2)}, u32[]{:S(2)}) collective-permute-start(bf16[768,1024]{1,0:T(8,128)(2,1)} %get-tuple-element.14), channel_id=1, source_target_pairs={{0,1},{1,0},{2,3},{3,2},{4,5},{5,4},{6,7},{7,6},{8,9},{9,8},{10,11... | collective-permute-start | bytes 4718600 | tf_op jit(solution)/shard_map/cond/branch_1_fun/ppermute | solution.py:56
  48.9 55.8 %collective-permute-start.9 = (bf16[784,640]{1,0:T(8,128)(2,1)}, bf16[784,640]{1,0:T(8,128)(2,1)}, u32[]{:S(2)}, u32[]{:S(2)}) collective-permute-start(bf16[784,640]{1,0:T(8,128)(2,1)} %get-tuple-element.47), channel_id=1, source_target_pairs={{0,3},{1,2},{2,1},{3,0},{4,7},{5,6},{6,5},{7,4},{8,11},{9,10},{10,... | collective-permute-start | bytes 3010568 | tf_op jit(solution)/shard_map/ppermute | solution.py:56
  48.9 36.8 %collective-permute-start.8 = (bf16[784,640]{1,0:T(8,128)(2,1)}, bf16[784,640]{1,0:T(8,128)(2,1)}, u32[]{:S(2)}, u32[]{:S(2)}) collective-permute-start(bf16[784,640]{1,0:T(8,128)(2,1)} %get-tuple-element.57), channel_id=1, source_target_pairs={{0,12},{1,13},{2,6},{3,7},{4,0},{5,1},{6,10},{7,11},{8,4},{9,5},{1... | collective-permute-start | bytes 3010568 | tf_op jit(solution)/shard_map/ppermute | solution.py:56
  61.7 43.0 %collective-permute-start.10 = (bf16[784,640]{1,0:T(8,128)(2,1)}, bf16[784,640]{1,0:T(8,128)(2,1)}, u32[]{:S(2)}, u32[]{:S(2)}) collective-permute-start(bf16[784,640]{1,0:T(8,128)(2,1)} %get-tuple-element.64), channel_id=1, source_target_pairs={{0,13},{1,12},{2,7},{3,6},{4,1},{5,0},{6,11},{7,10},{8,5},{9,4},{1... | collective-permute-start | bytes 3010568 | tf_op jit(solution)/shard_map/ppermute | solution.py:56
  64.2 61.6 %collective-permute-start.11 = (bf16[784,640]{1,0:T(8,128)(2,1)}, bf16[784,640]{1,0:T(8,128)(2,1)}, u32[]{:S(2)}, u32[]{:S(2)}) collective-permute-start(bf16[784,640]{1,0:T(8,128)(2,1)} %get-tuple-element.67), channel_id=1, source_target_pairs={{0,3},{1,2},{2,1},{3,0},{4,7},{5,6},{6,5},{7,4},{8,11},{9,10},{10,... | collective-permute-start | bytes 3010568 | tf_op jit(solution)/shard_map/ppermute | solution.py:56
  85.7 40.1 %collective-permute-start.12 = (bf16[784,640]{1,0:T(8,128)(2,1)}, bf16[784,640]{1,0:T(8,128)(2,1)}, u32[]{:S(2)}, u32[]{:S(2)}) collective-permute-start(bf16[784,640]{1,0:T(8,128)(2,1)} %get-tuple-element.68), channel_id=1, source_target_pairs={{0,13},{1,12},{2,7},{3,6},{4,1},{5,0},{6,11},{7,10},{8,5},{9,4},{1... | collective-permute-start | bytes 3010568 | tf_op jit(solution)/shard_map/ppermute | solution.py:56
  104.7 0.9 copy-start
  105.6 0.7 copy-start.1
  134.1 5.7 %collective-permute-start.13 = (f32[48,96]{1,0:T(8,128)S(1)}, f32[48,96]{1,0:T(8,128)S(1)}, u32[]{:S(2)}, u32[]{:S(2)}) collective-permute-start(f32[48,96]{1,0:T(8,128)S(1)} %get-tuple-element.70), channel_id=1, source_target_pairs={{0,4},{1,5},{2,14},{3,15},{4,8},{5,9},{6,2},{7,3},{8,12},{9,13},{1... | collective-permute-start | bytes 55304 | tf_op jit(solution)/shard_map/ppermute | solution.py:56
  134.2 7.4 %collective-permute-start.14 = (f32[48,96]{1,0:T(8,128)S(1)}, f32[48,96]{1,0:T(8,128)S(1)}, u32[]{:S(2)}, u32[]{:S(2)}) collective-permute-start(f32[48,96]{1,0:T(8,128)S(1)} %get-tuple-element.71), channel_id=1, source_target_pairs={{0,5},{1,4},{2,15},{3,14},{4,9},{5,8},{6,3},{7,2},{8,13},{9,12},{1... | collective-permute-start | bytes 55304 | tf_op jit(solution)/shard_map/ppermute | solution.py:56
  137.0 4.7 %collective-permute-start.15 = (f32[48,96]{1,0:T(8,128)S(1)}, f32[48,96]{1,0:T(8,128)S(1)}, u32[]{:S(2)}, u32[]{:S(2)}) collective-permute-start(f32[48,96]{1,0:T(8,128)S(1)} %get-tuple-element.72), channel_id=1, source_target_pairs={{0,2},{1,3},{2,0},{3,1},{4,6},{5,7},{6,4},{7,5},{8,10},{9,11},{10,... | collective-permute-start | bytes 55304 | tf_op jit(solution)/shard_map/ppermute | solution.py:56
  138.3 3.3 %collective-permute-start.16 = (f32[48,96]{1,0:T(8,128)S(1)}, f32[48,96]{1,0:T(8,128)S(1)}, u32[]{:S(2)}, u32[]{:S(2)}) collective-permute-start(f32[48,96]{1,0:T(8,128)S(1)} %get-tuple-element.73), channel_id=1, source_target_pairs={{0,3},{1,2},{2,1},{3,0},{4,7},{5,6},{6,5},{7,4},{8,11},{9,10},{10,... | collective-permute-start | bytes 55304 | tf_op jit(solution)/shard_map/ppermute | solution.py:56
  138.7 2.9 %collective-permute-start.17 = (f32[48,96]{1,0:T(8,128)S(1)}, f32[48,96]{1,0:T(8,128)S(1)}, u32[]{:S(2)}, u32[]{:S(2)}) collective-permute-start(f32[48,96]{1,0:T(8,128)S(1)} %get-tuple-element.74), channel_id=1, source_target_pairs={{0,1},{1,0},{2,3},{3,2},{4,5},{5,4},{6,7},{7,6},{8,9},{9,8},{10,11... | collective-permute-start | bytes 55304 | tf_op jit(solution)/shard_map/ppermute | solution.py:56
